TPU v7x, 32 devices: a whole 2x2x4 slice. The times are simulated.
32 devices in a mesh: run: 2 (over y), tile: 4 (over z), site: 2 (over x), freq: 2 (over core).
Axes of the slice: x: 2, y: 2, z: 4, core: 2. Of those that a mesh axis runs over, the one named last changes fastest.
Arguments:
- jacobian: bfloat16 [256, 16, 8, 8, 128], P(('run', 'tile', 'site'), None, 'freq'), parts along dimension 0, may hold values from -6 to 6
- footprint: int32 [256, 16], P(('run', 'tile', 'site')), parts along dimension 0, may hold values from 0 to 4095, as said below
- home: int32 [8192], P('run'), parts along dimension 0, may hold values from 0 to 4095, as said below
- residual: float32 [256, 8, 8], P(('run', 'tile', 'site'), 'freq'), parts along dimension 0, may hold values from -6 to 6
- weights: float32 [256], P(('run', 'tile', 'site')), parts along dimension 0, may hold values from 0.2 to 2
- damping: float32 [8192, 128], P(('run', 'tile', 'site')), parts along dimension 0, may hold values from 2 to 50
- step_lengths: float32 [8], replicated, may hold values from 0.2 to 1.2
Outputs:
- model_step: float32 [8192, 128], P(('run', 'tile', 'site')), parts along dimension 0
- change: float32 [256, 8, 8], P(('run', 'tile', 'site'), 'freq'), parts along dimension 0
- curve: float32 [16, 8], P(('run', 'freq')), parts along dimension 0
There are 2 independent parts, one for each index of `run`. A program takes and returns all parts, laid end to end along the dimension named above; an argument that names none is the same for every part. Nothing has to cross between parts.
Inputs may be any that keep to these rules, and one draw needn't show every extreme that they name: home is a permutation of 0 to 4095. `footprint`: of the 256 entries of each aligned block of 16 sites, at most 64 have home[block] // 512 equal to any one value; one value receives exactly 64 entries from every such block.
All inputs are finite; a program needn't handle non-finite values.
Results may differ from a plain program's by a relative error of at most 0.0029.
Values may be sent and summed in bfloat16 or wider, within the bound.
A program may use at most 64 MiB of HBM per device.

v0:
```python
import jax
import jax.numpy as jnp
from jax import lax
from jax.sharding import PartitionSpec as P


def shards(jacobian, footprint, home, residual, weights, damping, step_lengths):
    site_count, foot_count, freq_local, comps, width = jacobian.shape
    blocks_dev = damping.shape[0]
    tiles = lax.axis_size("tile")
    groups = lax.axis_size("site")
    owner_count = tiles * groups
    entries = site_count * foot_count
    capacity = 2 * entries // owner_count
    weighted = (weights[:, None, None] * residual).astype(jnp.bfloat16)
    grad_terms = jnp.einsum(
        "skfcb,sfc->skb", jacobian, weighted, preferred_element_type=jnp.float32
    )
    curve_terms = weights[:, None, None] * jnp.sum(
        jnp.square(jacobian.astype(jnp.float32)), axis=(2, 3)
    )
    terms = jnp.concatenate([grad_terms, curve_terms], axis=-1).reshape(entries, 2 * width)
    position = home[footprint.reshape(-1)]
    dest_rank = position // blocks_dev
    local_slot = position % blocks_dev
    member = (dest_rank[:, None] == jnp.arange(owner_count, dtype=jnp.int32)[None, :]).astype(
        jnp.int32
    )
    earlier = jnp.cumsum(member, axis=0) - member
    order_in = jnp.sum(earlier * member, axis=1)
    bucket = dest_rank * capacity + order_in
    outgoing = jnp.zeros((owner_count * capacity, 2 * width), jnp.float32).at[bucket].set(terms)
    out_slots = (
        jnp.full((owner_count * capacity,), blocks_dev, jnp.int32).at[bucket].set(local_slot)
    )
    received, in_slots = (
        lax.all_to_all(
            outgoing.reshape(owner_count, capacity, 2 * width),
            ("tile", "site"),
            split_axis=0,
            concat_axis=0,
            tiled=True,
        ),
        lax.all_to_all(
            out_slots.reshape(owner_count, capacity),
            ("tile", "site"),
            split_axis=0,
            concat_axis=0,
            tiled=True,
        ),
    )
    flat_slots = in_slots.reshape(-1)
    totals = jax.ops.segment_sum(
        received.reshape(-1, 2 * width), flat_slots, num_segments=blocks_dev + 1
    )[:blocks_dev]
    totals = lax.psum(totals, "freq")
    model_step = totals[:, :width] / (totals[:, width:] + damping)
    step_low = jnp.concatenate(
        [model_step.astype(jnp.bfloat16), jnp.zeros((1, width), jnp.bfloat16)], axis=0
    )
    reply = step_low[flat_slots]
    returned = lax.all_to_all(
        reply.reshape(owner_count, capacity, width),
        ("tile", "site"),
        split_axis=0,
        concat_axis=0,
        tiled=True,
    )
    entry_rows = returned.reshape(owner_count * capacity, width)[bucket]
    entry_step = entry_rows.reshape(site_count, foot_count, width)
    change = jnp.einsum("skfcb,skb->sfc", jacobian, entry_step, preferred_element_type=jnp.float32)
    scale_total = site_count * owner_count * comps
    gap = residual[:, :, :, None] - step_lengths[None, None, None, :] * change[:, :, :, None]
    partial_sum = jnp.einsum("s,sfca->fa", weights, gap * gap)
    curve = lax.psum(partial_sum, ("tile", "site")) / scale_total
    return (model_step, change, curve)


def solution(mesh):
    placed = (
        P(("run", "tile", "site"), None, "freq", None, None),
        P(("run", "tile", "site"), None),
        P("run"),
        P(("run", "tile", "site"), "freq", None),
        P(("run", "tile", "site")),
        P(("run", "tile", "site"), None),
        P(),
    )
    return jax.shard_map(
        shards,
        mesh=mesh,
        in_specs=placed,
        out_specs=(
            P(("run", "tile", "site"), None),
            P(("run", "tile", "site"), "freq", None),
            P(("run", "freq"), None),
        ),
        check_vma=False,
    )
```

profile of v0, /device:TPU:0, one launch (start us, length us, event | category | flops | bytes accessed | tf_op | source)
XLA Modules:
  0.0 117.0 jit_solution(13052791357690887810)
XLA Ops:
  7.2 0.9 reshape.181
  8.2 1.7 %gather_fusion = s32[256]{0:T(256)S(1)} fusion(s32[4096]{0:T(1024)S(1)} %copy-done, s32[1024]{0:T(1024)S(1)} %pad_clamp_fusion.2), kind=kCustom, calls=%fused_computation | custom fusion | bytes 3072 | tf_op jit(solution)/shard_map/gather | solution.py:23
  9.9 0.6 reduce-window.6
  10.5 0.2 slice_reduce_fusion
  10.8 0.1 fusion.10
  10.9 1.4 %scatter_custom_fusion = s32[512]{0:T(512)S(1)} fusion(s32[256]{0:T(256)S(1)} %bitcast.64, s32[256]{0:T(256)S(1)} %get-tuple-element.5, s32[]{:T(128)} %constant.41.clone.1), kind=kCustom, calls=%fused_computation.49 | custom fusion | bytes 2052 | tf_op jit(solution)/shard_map/scatter | solution.py:34
  12.3 0.7 all_to_all.12
  13.0 7.3 %all-to-all-start = ((s32[8,1,64]{2,1,0:T(1,128)}), s32[8,1,64]{2,1,0:T(1,128)S(1)}, u32[]{:S(2)}, u32[]{:S(2)}) async-start(s32[8,1,64]{2,1,0:T(1,128)} %all_to_all.12), calls=%async_computation | async-start | bytes 8192 | tf_op jit(solution)/shard_map/all_to_all | solution.py:44
  20.2 2.3 %multiply_reduce_fusion = f32[16,16,128]{2,1,0:T(8,128)S(1)} fusion(bf16[16,16,4,8,128]{4,3,2,1,0:T(8,128)(2,1)} %param.7), kind=kLoop, calls=%fused_computation.6 | loop fusion | flops 3112960 | bytes 2228224 | tf_op jit(solution)/shard_map/reduce_sum | solution.py:19
  22.6 0.1 broadcast_multiply_fusion
  22.7 0.1 copy.14
  22.8 0.6 fusion.22
  23.4 2.2 %scatter_custom_fusion.1 = f32[512,256]{1,0:T(8,128)} fusion(s32[256]{0:T(256)S(1)} %bitcast.65, f32[256,256]{1,0:T(8,128)S(1)} %bitcast.56, f32[]{:T(128)} %constant.40.clone.1), kind=kCustom, calls=%fused_computation.14 | custom fusion | bytes 524292 | tf_op jit(solution)/shard_map/scatter | solution.py:32
  25.6 1.0 all-to-all-done
  26.6 5.0 %all-to-all-start.1 = ((f32[8,64,256]{2,1,0:T(8,128)}), f32[8,64,256]{2,1,0:T(8,128)S(1)}, u32[]{:S(2)}, u32[]{:S(2)}) async-start(f32[8,64,256]{2,1,0:T(8,128)} %bitcast.11), calls=%async_computation.1 | async-start | bytes 1048576 | tf_op jit(solution)/shard_map/all_to_all | solution.py:37
  31.7 0.5 broadcast.204
  32.2 0.7 reduce.7
  32.9 12.7 %all-to-all-done.1 = f32[8,64,256]{2,1,0:T(8,128)S(1)} async-done(((f32[8,64,256]{2,1,0:T(8,128)}), f32[8,64,256]{2,1,0:T(8,128)S(1)}, u32[]{:S(2)}, u32[]{:S(2)}) %all-to-all-start.1) | async-done | bytes 524320 | tf_op jit(solution)/shard_map/all_to_all | solution.py:37
  45.6 3.7 %scatter_custom_fusion.2 = f32[513,256]{1,0:T(8,128)S(1)} fusion(s32[512]{0:T(512)S(1)} %reshape.231, f32[512,256]{1,0:T(8,128)S(1)} %bitcast.54, f32[]{:T(128)} %constant.40.clone.1), kind=kCustom, calls=%fused_computation.9 | custom fusion | flops 131072 | bytes 525316 | tf_op jit(solution)/shard_map/scatter-add | solution.py:53
  49.3 0.8 slice.27
  50.2 17.9 %all-reduce.3.cloned.1.call-done = f32[512,256]{1,0:T(8,128)} async-done(((f32[512,256]{1,0:T(8,128)}), f32[512,256]{1,0:T(8,128)}) %all-reduce.3.cloned.1.call-update) | async-done | bytes 524304 | tf_op jit(solution)/shard_map/psum | solution.py:56
  68.1 1.8 %fusion.17 = (bf16[512,128]{1,0:T(8,128)(2,1)S(1)}, f32[512,128]{1,0:T(8,128)}) fusion(f32[512,128]{1,0:T(8,128)S(1)} %copy-done.2, f32[512,256]{1,0:T(8,128)} %all-reduce.3.cloned.1.call-done), kind=kLoop, calls=%fused_computation.55 | loop fusion | flops 196608 | bytes 1179648 | tf_op jit(solution)/shard_map/convert_element_type | solution.py:59
  69.9 1.9 %gather_fusion.1 = bf16[512,128]{1,0:T(8,128)(2,1)} fusion(bf16[513,128]{1,0:T(8,128)(2,1)S(1)} %concatenate.7, s32[1024]{0:T(1024)S(1)} %pad_clamp_fusion.1), kind=kCustom, calls=%fused_computation.1 | custom fusion | bytes 264192 | tf_op jit(solution)/shard_map/gather | solution.py:61
  71.8 5.8 %all-to-all-start.2 = ((bf16[8,64,128]{2,1,0:T(8,128)(2,1)}), bf16[8,64,128]{2,1,0:T(8,128)(2,1)S(1)}, u32[]{:S(2)}, u32[]{:S(2)}) async-start(bf16[8,64,128]{2,1,0:T(8,128)(2,1)} %bitcast.14), calls=%async_computation.2 | async-start | bytes 262144 | tf_op jit(solution)/shard_map/all_to_all | solution.py:62
  77.6 7.4 %all-to-all-done.2 = bf16[8,64,128]{2,1,0:T(8,128)(2,1)S(1)} async-done(((bf16[8,64,128]{2,1,0:T(8,128)(2,1)}), bf16[8,64,128]{2,1,0:T(8,128)(2,1)S(1)}, u32[]{:S(2)}, u32[]{:S(2)}) %all-to-all-start.2) | async-done | bytes 131104 | tf_op jit(solution)/shard_map/all_to_all | solution.py:62
  85.1 0.9 gather_fusion.2
  85.9 4.7 %fusion = f32[16,1,4,8,1]{3,1,4,2,0:T(1,128)S(1)} fusion(bf16[16,16,4,8,128]{4,3,2,1,0:T(8,128)(2,1)S(1)} %copy-done.1, bf16[16,16,128,1,1]{2,1,0,3,4:T(8,128)(2,1)S(1)} %bitcast.57), kind=kOutput, calls=%fused_computation.7 | convolution fusion | flops 2097152 | bytes 2164736 | tf_op jit(solution)/shard_map/skfcb,skb->sfc/dot_general | solution.py:71
  90.6 0.1 copy.18
  90.7 0.1 multiply_reduce_fusion.1
  90.8 0.1 fusion.19
  91.0 18.6 %psum.15 = f32[4,8]{1,0:T(4,128)S(1)} all-reduce(f32[4,8]{1,0:T(4,128)S(1)} %bitcast.63), channel_id=1, replica_groups=mesh['run'=2,'tile'=4,'site'=2,'freq'=2] {'tile','site'}, use_global_device_ids=true, to_apply=%region_9.10 | all-reduce | flops 32 | bytes 256 | tf_op jit(solution)/shard_map/psum | solution.py:75
  109.5 0.6 broadcast_multiply_fusion.1
  (32 shorter events, 0.4 us)
Async XLA Ops:
  7.2 1.0 copy-start
  7.2 15.6 %copy-start.1 = (bf16[16,16,4,8,128]{4,3,2,1,0:T(8,128)(2,1)S(1)}, bf16[16,16,4,8,128]{4,3,2,1,0:T(8,128)(2,1)}, u32[]{:S(2)}) copy-start(bf16[16,16,4,8,128]{4,3,2,1,0:T(8,128)(2,1)} %param.7) | copy-start | bytes 6291460
  7.2 15.4 %copy-start.5 = (f32[16]{0:T(128)S(1)}, f32[16]{0:T(128)}, u32[]{:S(2)}) copy-start(f32[16]{0:T(128)} %param.11) | copy-start | bytes 196
  7.2 15.5 %copy-start.4 = (f32[16,4,8]{0,2,1:T(8,128)S(1)}, f32[16,4,8]{0,2,1:T(8,128)}, u32[]{:S(2)}) copy-start(f32[16,4,8]{0,2,1:T(8,128)} %param.10) | copy-start | bytes 6148
  13.0 13.6 %all-to-all-start = ((s32[8,1,64]{2,1,0:T(1,128)}), s32[8,1,64]{2,1,0:T(1,128)S(1)}, u32[]{:S(2)}, u32[]{:S(2)}) async-start(s32[8,1,64]{2,1,0:T(1,128)} %all_to_all.12), calls=%async_computation | async-start | bytes 8192 | tf_op jit(solution)/shard_map/all_to_all | solution.py:44
  23.4 44.7 %copy-start.2 = (f32[512,128]{1,0:T(8,128)S(1)}, f32[512,128]{1,0:T(8,128)}, u32[]{:S(2)}) copy-start(f32[512,128]{1,0:T(8,128)} %param.12) | copy-start | bytes 786436
  26.6 19.0 %all-to-all-start.1 = ((f32[8,64,256]{2,1,0:T(8,128)}), f32[8,64,256]{2,1,0:T(8,128)S(1)}, u32[]{:S(2)}, u32[]{:S(2)}) async-start(f32[8,64,256]{2,1,0:T(8,128)} %bitcast.11), calls=%async_computation.1 | async-start | bytes 1048576 | tf_op jit(solution)/shard_map/all_to_all | solution.py:37
  31.6 36.5 %all-reduce.3.cloned.1.call-start = ((), (), s32[]{:S(2)}) async-start(), calls=%async_computation.3 | async-start | bytes 1048576 | tf_op jit(solution)/shard_map/psum | solution.py:56
  71.8 13.2 %all-to-all-start.2 = ((bf16[8,64,128]{2,1,0:T(8,128)(2,1)}), bf16[8,64,128]{2,1,0:T(8,128)(2,1)S(1)}, u32[]{:S(2)}, u32[]{:S(2)}) async-start(bf16[8,64,128]{2,1,0:T(8,128)(2,1)} %bitcast.14), calls=%async_computation.2 | async-start | bytes 262144 | tf_op jit(solution)/shard_map/all_to_all | solution.py:62
  85.1 5.6 %copy-start.6 = (f32[8]{0:T(128)S(1)}, f32[8]{0:T(128)}, u32[]{:S(2)}) copy-start(f32[8]{0:T(128)} %param.13) | copy-start | bytes 100
  90.7 19.4 %copy-start.3 = (f32[16,1,4,8,1]{0,3,2,1,4:T(8,128)}, f32[16,1,4,8,1]{0,3,2,1,4:T(8,128)S(1)}, u32[]{:S(2)}) copy-start(f32[16,1,4,8,1]{0,3,2,1,4:T(8,128)S(1)} %copy.18) | copy-start | bytes 6148
Sparse Core Ops, SparseCore 0:
  50.3 17.8 all-reduce.2
where the time goes:
time: 117 us
  waiting for transfers between devices  39 us (33%)
  blocking collectives  18.6 us (16%)
  starting transfers between devices  18.1 us (15%)
  between operations  14.2 us (12%)
  local copies, waits for them, and re-layouts  11.6 us (10%)
  other arithmetic  10.1 us (9%)
  matrix products  5.41 us (5%)
    psum x1, blocking collectives, shards(): curve = lax.psum(partial_sum, ('tile', 'site')) / scale_total  18.6 us
    psum x1, waiting for transfers between devices, shards(): totals = lax.psum(totals, 'freq')  17.9 us
    all_to_all x1, waiting for transfers between devices, shards(): lax.all_to_all(outgoing.reshape(owner_count, capacity, 2 * width), ('tile...  12.7 us
    all_to_all x1, waiting for transfers between devices, shards(): lax.all_to_all(reply.reshape(owner_count, capacity, width), ('tile', 'sit...  7.43 us
    all_to_all x1, starting transfers between devices, shards(): lax.all_to_all(out_slots.reshape(owner_count, capacity), ('tile', 'site')...  7.25 us
    all_to_all x1, starting transfers between devices, shards(): lax.all_to_all(reply.reshape(owner_count, capacity, width), ('tile', 'sit...  5.78 us
    all_to_all x1, starting transfers between devices, shards(): lax.all_to_all(outgoing.reshape(owner_count, capacity, 2 * width), ('tile...  5 us
    dot_general x1, matrix products, shards(): jnp.einsum('skfcb,skb->sfc', jacobian, entry_step, preferred_element_type...  4.69 us
  transfers between devices with their start and end apart: 4, of which 4 were waited for; matrix products, arithmetic and copies ran while one was open for 6% of the time, Pallas kernels for 0%

commit v1 on v0

--- a/solution.py
+++ b/solution.py
@@ -72,7 +72,7 @@
     scale_total = site_count * owner_count * comps
     gap = residual[:, :, :, None] - step_lengths[None, None, None, :] * change[:, :, :, None]
     partial_sum = jnp.einsum("s,sfca->fa", weights, gap * gap)
-    curve = lax.psum(partial_sum, ("tile", "site")) / scale_total
+    curve = jnp.sum(lax.all_gather(partial_sum, ("tile", "site")), axis=0) / scale_total
     return (model_step, change, curve)
 
 

time: 117 us -> 125 us (1.068)
  blocking collectives: 18.6 us -> 26 us
    all_gather x0 -> x1, blocking collectives: none -> 26 us  [shards(): lax.all_gather(partial_sum, ('tile', 'site'))]
    psum x1 -> x0, blocking collectives: 18.6 us -> none  [shards(): curve = lax.psum(partial_sum, ('tile', 'site')) / scale_total]
  transfers between devices with their start and end apart: 4 -> 4, of which waited for: 4 -> 4; matrix products, arithmetic and copies ran while one was open for 6% -> 5% of each run, Pallas kernels for 0% -> 0%
where the time goes in v1:
time: 125 us; the launch traced here: 124 us
  waiting for transfers between devices  39 us (31%)
  blocking collectives  26 us (21%)
  starting transfers between devices  18.1 us (14%)
  between operations  14.2 us (11%)
  local copies, waits for them, and re-layouts  11.6 us (9%)
  other arithmetic  10.1 us (8%)
  matrix products  5.41 us (4%)
    all_gather x1, blocking collectives, shards(): lax.all_gather(partial_sum, ('tile', 'site'))  26 us
    psum x1, waiting for transfers between devices, shards(): totals = lax.psum(totals, 'freq')  17.9 us
    all_to_all x1, waiting for transfers between devices, shards(): lax.all_to_all(outgoing.reshape(owner_count, capacity, 2 * width), ('tile...  12.7 us
    all_to_all x1, waiting for transfers between devices, shards(): lax.all_to_all(reply.reshape(owner_count, capacity, width), ('tile', 'sit...  7.43 us
    all_to_all x1, starting transfers between devices, shards(): lax.all_to_all(out_slots.reshape(owner_count, capacity), ('tile', 'site')...  7.25 us
    all_to_all x1, starting transfers between devices, shards(): lax.all_to_all(reply.reshape(owner_count, capacity, width), ('tile', 'sit...  5.78 us
    all_to_all x1, starting transfers between devices, shards(): lax.all_to_all(outgoing.reshape(owner_count, capacity, 2 * width), ('tile...  5 us
    dot_general x1, matrix products, shards(): jnp.einsum('skfcb,skb->sfc', jacobian, entry_step, preferred_element_type...  4.69 us
  transfers between devices with their start and end apart: 4, of which 4 were waited for; matrix products, arithmetic and copies ran while one was open for 5% of the time, Pallas kernels for 0%

profile of v1, /device:TPU:0, one launch (start us, length us, event | category | flops | bytes accessed | tf_op | source)
XLA Modules:
  0.0 124.4 jit_solution(11161359256297389192)
XLA Ops:
  7.2 0.9 reshape.181
  8.2 1.7 %gather_fusion = s32[256]{0:T(256)S(1)} fusion(s32[4096]{0:T(1024)S(1)} %copy-done, s32[1024]{0:T(1024)S(1)} %pad_clamp_fusion.2), kind=kCustom, calls=%fused_computation | custom fusion | bytes 3072 | tf_op jit(solution)/shard_map/gather | solution.py:23
  9.9 0.6 reduce-window.6
  10.5 0.2 slice_reduce_fusion
  10.8 0.1 fusion.10
  10.9 1.4 %scatter_custom_fusion = s32[512]{0:T(512)S(1)} fusion(s32[256]{0:T(256)S(1)} %bitcast.65, s32[256]{0:T(256)S(1)} %get-tuple-element.5, s32[]{:T(128)} %constant.41.clone.1), kind=kCustom, calls=%fused_computation.49 | custom fusion | bytes 2052 | tf_op jit(solution)/shard_map/scatter | solution.py:34
  12.3 0.7 all_to_all.12
  13.0 7.3 %all-to-all-start = ((s32[8,1,64]{2,1,0:T(1,128)}), s32[8,1,64]{2,1,0:T(1,128)S(1)}, u32[]{:S(2)}, u32[]{:S(2)}) async-start(s32[8,1,64]{2,1,0:T(1,128)} %all_to_all.12), calls=%async_computation | async-start | bytes 8192 | tf_op jit(solution)/shard_map/all_to_all | solution.py:44
  20.2 2.3 %multiply_reduce_fusion = f32[16,16,128]{2,1,0:T(8,128)S(1)} fusion(bf16[16,16,4,8,128]{4,3,2,1,0:T(8,128)(2,1)} %param.7), kind=kLoop, calls=%fused_computation.6 | loop fusion | flops 3112960 | bytes 2228224 | tf_op jit(solution)/shard_map/reduce_sum | solution.py:19
  22.6 0.1 broadcast_multiply_fusion
  22.7 0.1 copy.16
  22.8 0.6 fusion.22
  23.4 2.2 %scatter_custom_fusion.1 = f32[512,256]{1,0:T(8,128)} fusion(s32[256]{0:T(256)S(1)} %bitcast.66, f32[256,256]{1,0:T(8,128)S(1)} %bitcast.57, f32[]{:T(128)} %constant.40.clone.1), kind=kCustom, calls=%fused_computation.14 | custom fusion | bytes 524292 | tf_op jit(solution)/shard_map/scatter | solution.py:32
  25.6 1.0 all-to-all-done
  26.6 5.0 %all-to-all-start.1 = ((f32[8,64,256]{2,1,0:T(8,128)}), f32[8,64,256]{2,1,0:T(8,128)S(1)}, u32[]{:S(2)}, u32[]{:S(2)}) async-start(f32[8,64,256]{2,1,0:T(8,128)} %bitcast.11), calls=%async_computation.1 | async-start | bytes 1048576 | tf_op jit(solution)/shard_map/all_to_all | solution.py:37
  31.7 0.5 broadcast.204
  32.2 0.7 reduce.8
  32.9 12.7 %all-to-all-done.1 = f32[8,64,256]{2,1,0:T(8,128)S(1)} async-done(((f32[8,64,256]{2,1,0:T(8,128)}), f32[8,64,256]{2,1,0:T(8,128)S(1)}, u32[]{:S(2)}, u32[]{:S(2)}) %all-to-all-start.1) | async-done | bytes 524320 | tf_op jit(solution)/shard_map/all_to_all | solution.py:37
  45.6 3.7 %scatter_custom_fusion.2 = f32[513,256]{1,0:T(8,128)S(1)} fusion(s32[512]{0:T(512)S(1)} %reshape.231, f32[512,256]{1,0:T(8,128)S(1)} %bitcast.55, f32[]{:T(128)} %constant.40.clone.1), kind=kCustom, calls=%fused_computation.9 | custom fusion | flops 131072 | bytes 525316 | tf_op jit(solution)/shard_map/scatter-add | solution.py:53
  49.3 0.8 slice.27
  50.2 17.9 %all-reduce.3.cloned.1.call-done = f32[512,256]{1,0:T(8,128)} async-done(((f32[512,256]{1,0:T(8,128)}), f32[512,256]{1,0:T(8,128)}) %all-reduce.3.cloned.1.call-update) | async-done | bytes 524304 | tf_op jit(solution)/shard_map/psum | solution.py:56
  68.1 1.8 %fusion.17 = (bf16[512,128]{1,0:T(8,128)(2,1)S(1)}, f32[512,128]{1,0:T(8,128)}) fusion(f32[512,128]{1,0:T(8,128)S(1)} %copy-done.2, f32[512,256]{1,0:T(8,128)} %all-reduce.3.cloned.1.call-done), kind=kLoop, calls=%fused_computation.55 | loop fusion | flops 196608 | bytes 1179648 | tf_op jit(solution)/shard_map/convert_element_type | solution.py:59
  69.9 1.9 %gather_fusion.1 = bf16[512,128]{1,0:T(8,128)(2,1)} fusion(bf16[513,128]{1,0:T(8,128)(2,1)S(1)} %concatenate.7, s32[1024]{0:T(1024)S(1)} %pad_clamp_fusion.1), kind=kCustom, calls=%fused_computation.1 | custom fusion | bytes 264192 | tf_op jit(solution)/shard_map/gather | solution.py:61
  71.8 5.8 %all-to-all-start.2 = ((bf16[8,64,128]{2,1,0:T(8,128)(2,1)}), bf16[8,64,128]{2,1,0:T(8,128)(2,1)S(1)}, u32[]{:S(2)}, u32[]{:S(2)}) async-start(bf16[8,64,128]{2,1,0:T(8,128)(2,1)} %bitcast.14), calls=%async_computation.2 | async-start | bytes 262144 | tf_op jit(solution)/shard_map/all_to_all | solution.py:62
  77.6 7.4 %all-to-all-done.2 = bf16[8,64,128]{2,1,0:T(8,128)(2,1)S(1)} async-done(((bf16[8,64,128]{2,1,0:T(8,128)(2,1)}), bf16[8,64,128]{2,1,0:T(8,128)(2,1)S(1)}, u32[]{:S(2)}, u32[]{:S(2)}) %all-to-all-start.2) | async-done | bytes 131104 | tf_op jit(solution)/shard_map/all_to_all | solution.py:62
  85.1 0.9 gather_fusion.2
  85.9 4.7 %fusion = f32[16,1,4,8,1]{3,1,4,2,0:T(1,128)S(1)} fusion(bf16[16,16,4,8,128]{4,3,2,1,0:T(8,128)(2,1)S(1)} %copy-done.1, bf16[16,16,128,1,1]{2,1,0,3,4:T(8,128)(2,1)S(1)} %bitcast.58), kind=kOutput, calls=%fused_computation.7 | convolution fusion | flops 2097152 | bytes 2164736 | tf_op jit(solution)/shard_map/skfcb,skb->sfc/dot_general | solution.py:71
  90.6 0.1 copy.20
  90.7 0.1 multiply_reduce_fusion.1
  90.8 0.1 fusion.19
  91.0 26.0 %all-gather.1 = f32[8,4,8]{2,1,0:T(4,128)S(1)} all-gather(f32[1,4,8]{2,1,0:T(4,128)S(1)} %bitcast.64), channel_id=2, replica_groups=mesh['run'=2,'tile'=4,'site'=2,'freq'=2] {'tile','site'}, dimensions={0}, use_global_device_ids=true | all-gather | bytes 1152 | tf_op jit(solution)/shard_map/all_gather | solution.py:75
  117.0 0.6 broadcast_multiply_fusion.1
  (33 shorter events, 0.4 us)
Async XLA Ops:
  7.2 1.0 copy-start
  7.2 15.6 %copy-start.1 = (bf16[16,16,4,8,128]{4,3,2,1,0:T(8,128)(2,1)S(1)}, bf16[16,16,4,8,128]{4,3,2,1,0:T(8,128)(2,1)}, u32[]{:S(2)}) copy-start(bf16[16,16,4,8,128]{4,3,2,1,0:T(8,128)(2,1)} %param.7) | copy-start | bytes 6291460
  7.2 15.4 %copy-start.5 = (f32[16]{0:T(128)S(1)}, f32[16]{0:T(128)}, u32[]{:S(2)}) copy-start(f32[16]{0:T(128)} %param.11) | copy-start | bytes 196
  7.2 15.5 %copy-start.4 = (f32[16,4,8]{0,2,1:T(8,128)S(1)}, f32[16,4,8]{0,2,1:T(8,128)}, u32[]{:S(2)}) copy-start(f32[16,4,8]{0,2,1:T(8,128)} %param.10) | copy-start | bytes 6148
  13.0 13.6 %all-to-all-start = ((s32[8,1,64]{2,1,0:T(1,128)}), s32[8,1,64]{2,1,0:T(1,128)S(1)}, u32[]{:S(2)}, u32[]{:S(2)}) async-start(s32[8,1,64]{2,1,0:T(1,128)} %all_to_all.12), calls=%async_computation | async-start | bytes 8192 | tf_op jit(solution)/shard_map/all_to_all | solution.py:44
  23.4 44.7 %copy-start.2 = (f32[512,128]{1,0:T(8,128)S(1)}, f32[512,128]{1,0:T(8,128)}, u32[]{:S(2)}) copy-start(f32[512,128]{1,0:T(8,128)} %param.12) | copy-start | bytes 786436
  26.6 19.0 %all-to-all-start.1 = ((f32[8,64,256]{2,1,0:T(8,128)}), f32[8,64,256]{2,1,0:T(8,128)S(1)}, u32[]{:S(2)}, u32[]{:S(2)}) async-start(f32[8,64,256]{2,1,0:T(8,128)} %bitcast.11), calls=%async_computation.1 | async-start | bytes 1048576 | tf_op jit(solution)/shard_map/all_to_all | solution.py:37
  31.6 36.5 %all-reduce.3.cloned.1.call-start = ((), (), s32[]{:S(2)}) async-start(), calls=%async_computation.3 | async-start | bytes 1048576 | tf_op jit(solution)/shard_map/psum | solution.py:56
  71.8 13.2 %all-to-all-start.2 = ((bf16[8,64,128]{2,1,0:T(8,128)(2,1)}), bf16[8,64,128]{2,1,0:T(8,128)(2,1)S(1)}, u32[]{:S(2)}, u32[]{:S(2)}) async-start(bf16[8,64,128]{2,1,0:T(8,128)(2,1)} %bitcast.14), calls=%async_computation.2 | async-start | bytes 262144 | tf_op jit(solution)/shard_map/all_to_all | solution.py:62
  85.1 5.6 %copy-start.6 = (f32[8]{0:T(128)S(1)}, f32[8]{0:T(128)}, u32[]{:S(2)}) copy-start(f32[8]{0:T(128)} %param.13) | copy-start | bytes 100
  90.7 26.9 %copy-start.3 = (f32[16,1,4,8,1]{0,3,2,1,4:T(8,128)}, f32[16,1,4,8,1]{0,3,2,1,4:T(8,128)S(1)}, u32[]{:S(2)}) copy-start(f32[16,1,4,8,1]{0,3,2,1,4:T(8,128)S(1)} %copy.20) | copy-start | bytes 6148
Sparse Core Ops, SparseCore 0:
  50.3 17.8 all-reduce.2
